TPU v7x, 32 devices: a whole 2x2x4 slice. The times are simulated.
32 devices in a mesh: row: 4 (over y, x), col: 8 (over z, core).
Axes of the slice: x: 2, y: 2, z: 4, core: 2. Of those that a mesh axis runs over, the one named last changes fastest.
Arguments:
- tiles: bfloat16 [256, 256, 256], P(('row', 'col')), may hold values from -0.09375 to 0.09375
- tile_rows: int32 [256], P(('row', 'col')), may hold values from 0 to 3, as said below
- tile_cols: int32 [256], P(('row', 'col')), may hold values from 0 to 1
- tile_count: int32 [32], P(('row', 'col')), may hold values from 0 to 8, as said below
- bounds: float32 [2], replicated, may hold values from -1 to 2, as said below
- vectors: float32 [4096, 128], P(('row', 'col')), may hold values from -6 to 6
Outputs:
- filtered: float32 [4096, 128], P(('row', 'col'))
- gram: float32 [128, 128], replicated
Inputs may be any that keep to these rules, and one draw needn't show every extreme that they name: `tile_rows`: within each device the first tile_count slots name distinct blocks with global block row I <= global block column J; the device's diagonal blocks (I = J) come first; every diagonal block of the Hamiltonian is stored; slots after the live ones hold valid indices but are not part of the matrix. `tile_count`: devices whose block rows all lie below their block columns have no live slot; some device has all 8 slots live. bounds[0] < -0.5 and bounds[1] > 1.0.
All inputs are finite; a program needn't handle non-finite values.
Results may differ from a plain program's by a relative error of at most 0.0037.
Values may be sent and summed in bfloat16 or wider, within the bound.
A program may use at most 64 MiB of HBM per device.

v0:
```python
import jax
import jax.numpy as jnp
from jax import lax
from jax.sharding import PartitionSpec as P

BLK_COL = 2


def spread(block, axis, holder):
    block = jnp.where(lax.axis_index(axis) == holder, block, jnp.zeros_like(block))
    return lax.psum(block, axis)


def on_device(tiles, tile_rows, tile_cols, tile_count, bounds, vectors):
    col_ratio = lax.axis_size("col") // lax.axis_size("row")
    col_index = lax.axis_index("col")
    row_index = lax.axis_index("row")
    root_row = col_index // col_ratio
    slot_total = tiles.shape[0]
    block_size = tiles.shape[1]
    share_rows = vectors.shape[0]
    width_vecs = vectors.shape[1]
    group_rows = share_rows * lax.axis_size("col")
    group_blocks = group_rows // block_size
    column_rows = BLK_COL * block_size
    total_rows = share_rows * lax.axis_size("row") * lax.axis_size("col")
    offset = col_index % col_ratio * column_rows
    live_mask = (jnp.arange(slot_total, dtype=jnp.int32) < tile_count[0]).astype(jnp.bfloat16)
    owner_flag = (row_index == root_row).astype(jnp.float32)
    center = (bounds[1] + bounds[0]) * 0.5
    halfwidth = (bounds[1] - bounds[0]) * 0.5

    def apply_hamiltonian(current_vec):
        vector_panel = current_vec.astype(jnp.bfloat16)
        row_panel = lax.all_gather(vector_panel, "col", axis=0, tiled=True)
        col_piece = lax.dynamic_slice_in_dim(row_panel, offset, column_rows, 0)
        col_panel = spread(col_piece, "row", root_row)
        row_input = row_panel.reshape(group_blocks, block_size, width_vecs)
        col_input = col_panel.reshape(BLK_COL, block_size, width_vecs)
        start_rows = jnp.zeros((group_blocks, block_size, width_vecs), jnp.float32)
        start_cols = jnp.zeros((BLK_COL, block_size, width_vecs), jnp.float32)
        masked_cols = col_input[tile_cols] * live_mask[:, None, None]
        masked_rows = row_input[tile_rows] * live_mask[:, None, None]
        forward = jnp.einsum("tab,tbk->tak", tiles, masked_cols, preferred_element_type=jnp.float32)
        backward = jnp.einsum(
            "tab,tak->tbk", tiles, masked_rows, preferred_element_type=jnp.float32
        )
        row_part = start_rows.at[tile_rows].add(forward)
        col_part = start_cols.at[tile_cols].add(backward)
        column_total = lax.psum(col_part, "row")
        row_part = row_part.reshape(group_rows, width_vecs)
        present = lax.dynamic_slice_in_dim(row_part, offset, column_rows, 0)
        updated = present + owner_flag * column_total.reshape(column_rows, width_vecs)
        row_part = lax.dynamic_update_slice_in_dim(row_part, updated, offset, 0)
        return lax.psum_scatter(row_part, "col", scatter_dimension=0, tiled=True)

    current_vec = (apply_hamiltonian(vectors) - center * vectors) / halfwidth
    image = apply_hamiltonian(current_vec)
    following = 2.0 * (image - center * current_vec) / halfwidth - vectors
    current_vec = following
    gram_local = lax.dot_general(
        current_vec,
        current_vec,
        (((0,), (0,)), ((), ())),
        precision=lax.Precision.HIGHEST,
        preferred_element_type=jnp.float32,
    )
    gram_total = lax.psum(gram_local, ("row", "col"))
    return (current_vec, gram_total / total_rows)


def solution(mesh):
    in_specs = (
        P(("row", "col"), None, None),
        P(("row", "col")),
        P(("row", "col")),
        P(("row", "col")),
        P(),
        P(("row", "col"), None),
    )
    out_specs = (P(("row", "col"), None), P())
    return jax.shard_map(
        on_device, mesh=mesh, in_specs=in_specs, out_specs=out_specs, check_vma=False
    )
```

profile of v0, /device:TPU:1, one launch (start us, length us, event | category | flops | bytes accessed | tf_op | source)
XLA Modules:
  0.0 414.4 jit_solution(1064199134010569408)
XLA Ops:
  7.2 0.9 convert_element_type.16
  8.2 15.8 %all_gather.6 = bf16[1024,128]{1,0:T(8,128)(2,1)S(1)} all-gather(bf16[128,128]{1,0:T(8,128)(2,1)S(1)} %convert_element_type.16), channel_id=1, replica_groups=mesh['row'=4,'col'=8] {'col'}, dimensions={0}, use_global_device_ids=true | all-gather | bytes 294912 | tf_op jit(solution)/shard_map/all_gather | solution.py:35
  23.9 0.7 dynamic-slice_select_fusion.1
  24.6 0.0 all-reduce.8.cloned.1.call-start
  25.4 0.6 copy-done.9
  26.0 0.6 gather_fusion.1
  26.7 0.4 convolution_bitcast_fusion.2
  27.1 0.3 copy.15
  27.4 0.3 copy-done.10
  27.8 1.3 scatter_fusion.1
  29.1 0.7 copy-done.4
  29.8 0.0 reduce-scatter.3.cloned.1.call-start
  29.9 37.0 %all-reduce.6.cloned.1.call-done = bf16[2,256,128]{2,1,0:T(8,128)(2,1)} async-done(((bf16[2,256,128]{2,1,0:T(8,128)(2,1)}), bf16[2,256,128]{2,1,0:T(8,128)(2,1)}) %all-reduce.6.cloned.1.call-update) | async-done | bytes 131088 | tf_op jit(solution)/shard_map/psum | solution.py:11
  66.9 1.5 gather_fusion
  68.5 1.7 convolution_bitcast_fusion.3
  70.2 1.5 copy.13
  71.8 1.3 scatter_fusion
  73.1 39.9 %all-reduce.8.cloned.1.call-done = f32[2,256,128]{2,1,0:T(8,128)} async-done(((f32[2,256,128]{2,1,0:T(8,128)}), f32[2,256,128]{2,1,0:T(8,128)}) %all-reduce.8.cloned.1.call-update) | async-done | bytes 262160 | tf_op jit(solution)/shard_map/psum | solution.py:50
  113.1 1.0 broadcast_multiply_fusion.1
  114.0 0.1 constant_dynamic-update-slice_fusion.1
  114.1 0.8 copy-done.2
  114.9 0.0 all-reduce.10.cloned.1.call-start
  114.9 0.6 fusion.9
  118.1 25.2 %reduce-scatter.3.cloned.1.call-done = f32[128,128]{1,0:T(8,128)} async-done(((f32[1024,128]{1,0:T(8,128)}), f32[128,128]{1,0:T(8,128)}) %reduce-scatter.3.cloned.1.call-update) | async-done | bytes 65552 | tf_op jit(solution)/shard_map/reduce_scatter | solution.py:55
  143.4 0.9 fusion.8
  144.2 18.0 %all_gather.7 = bf16[1024,128]{1,0:T(8,128)(2,1)S(1)} all-gather(bf16[128,128]{1,0:T(8,128)(2,1)S(1)} %fusion.8), channel_id=1, replica_groups=mesh['row'=4,'col'=8] {'col'}, dimensions={0}, use_global_device_ids=true | all-gather | bytes 294912 | tf_op jit(solution)/shard_map/all_gather | solution.py:35
  162.3 0.7 dynamic-slice_select_fusion
  162.9 0.6 gather_fusion.3
  163.6 0.0 all-reduce.12.cloned.1.call-start
  163.7 0.4 convolution_bitcast_fusion
  164.1 0.3 copy.19
  164.4 1.3 scatter_fusion.3
  165.8 0.7 copy-done.3
  166.5 0.0 reduce-scatter.5.cloned.1.call-start
  166.6 36.5 %all-reduce.10.cloned.1.call-done = bf16[2,256,128]{2,1,0:T(8,128)(2,1)} async-done(((bf16[2,256,128]{2,1,0:T(8,128)(2,1)}), bf16[2,256,128]{2,1,0:T(8,128)(2,1)}) %all-reduce.10.cloned.1.call-update) | async-done | bytes 131088 | tf_op jit(solution)/shard_map/psum | solution.py:11
  203.1 1.5 gather_fusion.2
  204.7 1.7 convolution_bitcast_fusion.1
  206.4 1.5 copy.17
  208.0 1.3 scatter_fusion.2
  209.3 39.5 %all-reduce.12.cloned.1.call-done = f32[2,256,128]{2,1,0:T(8,128)} async-done(((f32[2,256,128]{2,1,0:T(8,128)}), f32[2,256,128]{2,1,0:T(8,128)}) %all-reduce.12.cloned.1.call-update) | async-done | bytes 262160 | tf_op jit(solution)/shard_map/psum | solution.py:50
  248.8 1.0 broadcast_multiply_fusion
  249.8 0.1 constant_dynamic-update-slice_fusion
  249.9 0.8 copy-done.1
  250.7 28.2 %reduce-scatter.5.cloned.1.call-done = f32[128,128]{1,0:T(8,128)} async-done(((f32[1024,128]{1,0:T(8,128)}), f32[128,128]{1,0:T(8,128)}) %reduce-scatter.5.cloned.1.call-update) | async-done | bytes 65552 | tf_op jit(solution)/shard_map/reduce_scatter | solution.py:55
  278.9 0.9 divide_subtract_fusion
  279.8 0.9 fusion.10
  280.8 125.3 %all-reduce.14.cloned.1.call-done = f32[128,128]{1,0:T(8,128)} async-done(((f32[128,128]{1,0:T(8,128)}), f32[128,128]{1,0:T(8,128)}) %all-reduce.14.cloned.1.call-update) | async-done | bytes 65552 | tf_op jit(solution)/shard_map/psum | solution.py:68
  406.1 1.5 broadcast_multiply_fusion.2
  (34 shorter events, 0.4 us)
Async XLA Ops:
  7.2 19.5 %copy-start = (bf16[8,256,256]{2,1,0:T(8,128)(2,1)S(1)}, bf16[8,256,256]{2,1,0:T(8,128)(2,1)}, u32[]{:S(2)}) copy-start(bf16[8,256,256]{2,1,0:T(8,128)(2,1)} %param.6) | copy-start | bytes 3145732
  7.2 59.8 %all-reduce.6.cloned.1.call-start = ((), (), s32[]{:S(2)}) async-start(), calls=%async_computation.2 | async-start | bytes 262144 | tf_op jit(solution)/shard_map/psum | solution.py:11
  24.6 88.4 %all-reduce.8.cloned.1.call-start = ((), (), s32[]{:S(2)}) async-start(), calls=%async_computation.3 | async-start | bytes 524288 | tf_op jit(solution)/shard_map/psum | solution.py:50
  25.3 0.7 copy-start.9
  27.1 0.7 copy-start.10
  29.1 0.7 copy-start.4
  29.8 113.5 %reduce-scatter.3.cloned.1.call-start = ((), (), s32[]{:S(2)}) async-start(), calls=%async_computation.4 | async-start | bytes 589824 | tf_op jit(solution)/shard_map/reduce_scatter | solution.py:55
  114.1 0.8 copy-start.2
  114.1 0.9 copy-start.8
  114.1 29.3 %copy-start.5 = (f32[128,128]{1,0:T(8,128)S(1)}, f32[128,128]{1,0:T(8,128)}, u32[]{:S(2)}) copy-start(f32[128,128]{1,0:T(8,128)} %param.11) | copy-start | bytes 196612
  114.9 88.2 %all-reduce.10.cloned.1.call-start = ((), (), s32[]{:S(2)}) async-start(), calls=%async_computation.5 | async-start | bytes 262144 | tf_op jit(solution)/shard_map/psum | solution.py:11
  163.6 85.2 %all-reduce.12.cloned.1.call-start = ((), (), s32[]{:S(2)}) async-start(), calls=%async_computation.6 | async-start | bytes 524288 | tf_op jit(solution)/shard_map/psum | solution.py:50
  165.8 0.7 copy-start.3
  166.5 112.4 %reduce-scatter.5.cloned.1.call-start = ((), (), s32[]{:S(2)}) async-start(), calls=%async_computation.7 | async-start | bytes 589824 | tf_op jit(solution)/shard_map/reduce_scatter | solution.py:55
  249.9 0.8 copy-start.1
  249.9 29.1 %copy-start.7 = (f32[128,128]{1,0:T(8,128)S(1)}, f32[128,128]{1,0:T(8,128)}, u32[]{:S(2)}) copy-start(f32[128,128]{1,0:T(8,128)} %reduce-scatter.3.cloned.1.call-done) | copy-start | bytes 196612
  250.7 155.4 %all-reduce.14.cloned.1.call-start = ((), (), s32[]{:S(2)}) async-start(), calls=%async_computation.8 | async-start | bytes 131072 | tf_op jit(solution)/shard_map/psum | solution.py:68
  279.8 0.9 copy-start.6
Sparse Core Ops, SparseCore 0:
  24.8 42.1 all-reduce.5
  70.1 42.8 all-reduce.7
  115.3 28.0 reduce-scatter.2
  163.7 39.3 all-reduce.9
  205.9 42.9 all-reduce.11
  251.0 27.8 reduce-scatter.4
  285.1 120.9 all-reduce.13
where the time goes:
time: 415 us; the launch traced here: 414 us
  waiting for transfers between devices  332 us (80%)
  blocking collectives  33.8 us (8%)
  between operations  17.7 us (4%)
  local copies, waits for them, and re-layouts  12.8 us (3%)
  other arithmetic  12.8 us (3%)
  matrix products  5.15 us (1%)
    psum x1, waiting for transfers between devices, on_device(): gram_total = lax.psum(gram_local, ('row', 'col'))  125 us
    psum x2, waiting for transfers between devices, apply_hamiltonian(): column_total = lax.psum(col_part, 'row')  79.5 us
    psum x2, waiting for transfers between devices, spread(): return lax.psum(block, axis)  73.6 us
    reduce_scatter x2, waiting for transfers between devices, apply_hamiltonian(): return lax.psum_scatter(row_part, 'col', scatter_dimension=0, tiled=True)  53.5 us
    all_gather x2, blocking collectives, apply_hamiltonian(): row_panel = lax.all_gather(vector_panel, 'col', axis=0, tiled=True)  33.8 us
  transfers between devices with their start and end apart: 7, of which 7 were waited for; matrix products, arithmetic and copies ran while one was open for 4% of the time, Pallas kernels for 0%

commit v1 on v0

--- a/solution.py
+++ b/solution.py
@@ -47,7 +47,11 @@
         )
         row_part = start_rows.at[tile_rows].add(forward)
         col_part = start_cols.at[tile_cols].add(backward)
-        column_total = lax.psum(col_part, "row")
+        column_total = col_part
+        for hop in (1, 2):
+            column_total = column_total + lax.ppermute(
+                column_total, "row", [(dev, dev ^ hop) for dev in range(4)]
+            )
         row_part = row_part.reshape(group_rows, width_vecs)
         present = lax.dynamic_slice_in_dim(row_part, offset, column_rows, 0)
         updated = present + owner_flag * column_total.reshape(column_rows, width_vecs)

time: 415 us -> 346 us (0.83)
  waiting for transfers between devices: 332 us -> 262 us
  starting transfers between devices: 0.29 us -> 5.1 us
    psum x2 -> x0, waiting for transfers between devices: 79.5 us -> none  [apply_hamiltonian(): column_total = lax.psum(col_part, 'row')]
    psum x2, waiting for transfers between devices: 73.6 us -> 80.3 us  [spread(): return lax.psum(block, axis)]
    ppermute x0 -> x4, starting transfers between devices: none -> 4.89 us  [apply_hamiltonian(): lax.ppermute(column_total, 'row', [(dev, dev ^ hop) for dev in range(4)])]
  transfers between devices with their start and end apart: 7 -> 9, of which waited for: 7 -> 7; matrix products, arithmetic and copies ran while one was open for 4% -> 4% of each run, Pallas kernels for 0% -> 0%
where the time goes in v1:
time: 346 us
  waiting for transfers between devices  262 us (76%)
  blocking collectives  33.9 us (10%)
  between operations  17.3 us (5%)
  other arithmetic  11.6 us (3%)
  local copies, waits for them, and re-layouts  10.8 us (3%)
  matrix products  5.13 us (1%)
  starting transfers between devices  5.1 us (1%)
    psum x1, waiting for transfers between devices, on_device(): gram_total = lax.psum(gram_local, ('row', 'col'))  125 us
    psum x2, waiting for transfers between devices, spread(): return lax.psum(block, axis)  80.3 us
    reduce_scatter x2, waiting for transfers between devices, apply_hamiltonian(): return lax.psum_scatter(row_part, 'col', scatter_dimension=0, tiled=True)  54.5 us
    all_gather x2, blocking collectives, apply_hamiltonian(): row_panel = lax.all_gather(vector_panel, 'col', axis=0, tiled=True)  33.9 us
  transfers between devices with their start and end apart: 9, of which 7 were waited for; matrix products, arithmetic and copies ran while one was open for 4% of the time, Pallas kernels for 0%

profile of v1, /device:TPU:1, one launch (start us, length us, event | category | flops | bytes accessed | tf_op | source)
XLA Modules:
  0.0 346.0 jit_solution(2220492196004717446)
XLA Ops:
  7.2 0.0 all-reduce.4.cloned.1.call-start
  7.2 0.7 compare_select_fusion.1
  8.0 0.8 convert_element_type.16
  8.8 15.8 %all_gather.6 = bf16[1024,128]{1,0:T(8,128)(2,1)S(1)} all-gather(bf16[128,128]{1,0:T(8,128)(2,1)S(1)} %convert_element_type.16), channel_id=1, replica_groups=mesh['row'=4,'col'=8] {'col'}, dimensions={0}, use_global_device_ids=true | all-gather | bytes 294912 | tf_op jit(solution)/shard_map/all_gather | solution.py:35
  25.2 0.6 gather_fusion.1
  25.9 0.4 convolution_bitcast_fusion.2
  26.4 0.3 copy.15
  26.7 0.3 copy-done.11
  27.0 1.3 scatter_fusion.1
  28.3 1.3 collective-permute-start
  29.6 0.7 dynamic-slice_select_fusion.1
  30.3 0.0 reduce-scatter.3.cloned.1.call-start
  30.4 41.6 %all-reduce.4.cloned.1.call-done = bf16[2,256,128]{2,1,0:T(8,128)(2,1)} async-done(((bf16[2,256,128]{2,1,0:T(8,128)(2,1)}), bf16[2,256,128]{2,1,0:T(8,128)(2,1)}) %all-reduce.4.cloned.1.call-update) | async-done | bytes 131088 | tf_op jit(solution)/shard_map/psum | solution.py:11
  72.0 1.5 gather_fusion
  73.6 1.1 collective-permute-start.1
  74.7 1.7 convolution_bitcast_fusion.3
  76.4 1.5 copy.13
  78.0 1.3 scatter_fusion
  79.4 1.0 collective-permute-done.1
  80.5 0.8 copy-done.2
  81.3 0.0 all-reduce.6.cloned.1.call-start
  81.3 0.6 fusion.9
  84.5 25.7 %reduce-scatter.3.cloned.1.call-done = f32[128,128]{1,0:T(8,128)} async-done(((f32[1024,128]{1,0:T(8,128)}), f32[128,128]{1,0:T(8,128)}) %reduce-scatter.3.cloned.1.call-update) | async-done | bytes 65552 | tf_op jit(solution)/shard_map/reduce_scatter | solution.py:59
  110.2 0.9 fusion.8
  111.1 18.2 %all_gather.7 = bf16[1024,128]{1,0:T(8,128)(2,1)S(1)} all-gather(bf16[128,128]{1,0:T(8,128)(2,1)S(1)} %fusion.8), channel_id=1, replica_groups=mesh['row'=4,'col'=8] {'col'}, dimensions={0}, use_global_device_ids=true | all-gather | bytes 294912 | tf_op jit(solution)/shard_map/all_gather | solution.py:35
  129.2 0.6 gather_fusion.3
  129.9 0.0 copy-done.5
  129.9 0.4 convolution_bitcast_fusion
  130.4 0.3 copy.19
  130.7 1.3 scatter_fusion.3
  132.0 1.3 collective-permute-start.2
  133.4 0.7 dynamic-slice_select_fusion
  134.1 0.0 reduce-scatter.5.cloned.1.call-start
  134.1 38.7 %all-reduce.6.cloned.1.call-done = bf16[2,256,128]{2,1,0:T(8,128)(2,1)} async-done(((bf16[2,256,128]{2,1,0:T(8,128)(2,1)}), bf16[2,256,128]{2,1,0:T(8,128)(2,1)}) %all-reduce.6.cloned.1.call-update) | async-done | bytes 131088 | tf_op jit(solution)/shard_map/psum | solution.py:11
  172.8 1.5 gather_fusion.2
  174.4 1.1 collective-permute-start.3
  175.6 1.7 convolution_bitcast_fusion.1
  177.3 1.5 copy.17
  178.9 1.3 scatter_fusion.2
  180.2 1.0 collective-permute-done.3
  181.3 0.8 copy-done.1
  182.1 0.0 all-reduce.8.cloned.1.call-start
  182.2 28.9 %reduce-scatter.5.cloned.1.call-done = f32[128,128]{1,0:T(8,128)} async-done(((f32[1024,128]{1,0:T(8,128)}), f32[128,128]{1,0:T(8,128)}) %reduce-scatter.5.cloned.1.call-update) | async-done | bytes 65552 | tf_op jit(solution)/shard_map/reduce_scatter | solution.py:59
  211.0 0.9 divide_subtract_fusion
  211.9 0.9 fusion.10
  212.8 0.0 all-reduce.8.cloned.1.call-update
  212.9 125.1 %all-reduce.8.cloned.1.call-done = f32[128,128]{1,0:T(8,128)} async-done(((f32[128,128]{1,0:T(8,128)}), f32[128,128]{1,0:T(8,128)}) %all-reduce.8.cloned.1.call-update) | async-done | bytes 65552 | tf_op jit(solution)/shard_map/psum | solution.py:72
  338.0 1.5 broadcast_multiply_fusion
  (40 shorter events, 0.5 us)
Async XLA Ops:
  7.2 18.7 %copy-start = (bf16[8,256,256]{2,1,0:T(8,128)(2,1)S(1)}, bf16[8,256,256]{2,1,0:T(8,128)(2,1)}, u32[]{:S(2)}) copy-start(bf16[8,256,256]{2,1,0:T(8,128)(2,1)} %param.6) | copy-start | bytes 3145732
  7.2 64.8 %all-reduce.4.cloned.1.call-start = ((), (), s32[]{:S(2)}) async-start(), calls=%async_computation.2 | async-start | bytes 262144 | tf_op jit(solution)/shard_map/psum | solution.py:11
  24.6 1.3 copy-start.3
  26.3 0.7 copy-start.11
  27.0 2.6 copy-start.4
  28.3 45.2 %collective-permute-start = (f32[2,256,128]{2,1,0:T(8,128)S(1)}, f32[2,256,128]{2,1,0:T(8,128)S(1)}, u32[]{:S(2)}, u32[]{:S(2)}) collective-permute-start(f32[2,256,128]{2,1,0:T(8,128)S(1)} %scatter_fusion.1), channel_id=1, source_target_pairs={{0,8},{8,0},{16,24},{24,16},{1,9},{9,1},{17,25},{25,17},{2,10},{10... | collective-permute-start | bytes 786440 | tf_op jit(solution)/shard_map/ppermute | solution.py:52
  30.3 79.9 %reduce-scatter.3.cloned.1.call-start = ((), (), s32[]{:S(2)}) async-start(), calls=%async_computation.3 | async-start | bytes 589824 | tf_op jit(solution)/shard_map/reduce_scatter | solution.py:59
  73.6 6.8 %collective-permute-start.1 = (f32[2,256,128]{2,1,0:T(8,128)S(1)}, f32[2,256,128]{2,1,0:T(8,128)S(1)}, u32[]{:S(2)}, u32[]{:S(2)}) collective-permute-start(f32[2,256,128]{2,1,0:T(8,128)S(1)} %add.69), channel_id=1, source_target_pairs={{0,16},{8,24},{16,0},{24,8},{1,17},{9,25},{17,1},{25,9},{2,18},{10... | collective-permute-start | bytes 786440 | tf_op jit(solution)/shard_map/ppermute | solution.py:52
  80.5 0.8 copy-start.2
  80.5 0.9 copy-start.10
  80.5 29.7 %copy-start.7 = (f32[128,128]{1,0:T(8,128)S(1)}, f32[128,128]{1,0:T(8,128)}, u32[]{:S(2)}) copy-start(f32[128,128]{1,0:T(8,128)} %param.11) | copy-start | bytes 196612
  81.3 91.5 %all-reduce.6.cloned.1.call-start = ((), (), s32[]{:S(2)}) async-start(), calls=%async_computation.4 | async-start | bytes 262144 | tf_op jit(solution)/shard_map/psum | solution.py:11
  129.2 0.7 copy-start.5
  130.7 2.7 copy-start.6
  132.0 42.3 %collective-permute-start.2 = (f32[2,256,128]{2,1,0:T(8,128)S(1)}, f32[2,256,128]{2,1,0:T(8,128)S(1)}, u32[]{:S(2)}, u32[]{:S(2)}) collective-permute-start(f32[2,256,128]{2,1,0:T(8,128)S(1)} %scatter_fusion.3), channel_id=1, source_target_pairs={{0,8},{8,0},{16,24},{24,16},{1,9},{9,1},{17,25},{25,17},{2,10},{10... | collective-permute-start | bytes 786440 | tf_op jit(solution)/shard_map/ppermute | solution.py:52
  134.1 76.9 %reduce-scatter.5.cloned.1.call-start = ((), (), s32[]{:S(2)}) async-start(), calls=%async_computation.5 | async-start | bytes 589824 | tf_op jit(solution)/shard_map/reduce_scatter | solution.py:59
  174.4 6.8 %collective-permute-start.3 = (f32[2,256,128]{2,1,0:T(8,128)S(1)}, f32[2,256,128]{2,1,0:T(8,128)S(1)}, u32[]{:S(2)}, u32[]{:S(2)}) collective-permute-start(f32[2,256,128]{2,1,0:T(8,128)S(1)} %add.73), channel_id=1, source_target_pairs={{0,16},{8,24},{16,0},{24,8},{1,17},{9,25},{17,1},{25,9},{2,18},{10... | collective-permute-start | bytes 786440 | tf_op jit(solution)/shard_map/ppermute | solution.py:52
  181.3 0.8 copy-start.1
  181.3 29.7 %copy-start.9 = (f32[128,128]{1,0:T(8,128)S(1)}, f32[128,128]{1,0:T(8,128)}, u32[]{:S(2)}) copy-start(f32[128,128]{1,0:T(8,128)} %reduce-scatter.3.cloned.1.call-done) | copy-start | bytes 196612
  182.1 155.8 %all-reduce.8.cloned.1.call-start = ((), (), s32[]{:S(2)}) async-start(), calls=%async_computation.6 | async-start | bytes 131072 | tf_op jit(solution)/shard_map/psum | solution.py:72
  211.9 0.9 copy-start.8
Sparse Core Ops, SparseCore 0:
  30.5 41.4 all-reduce.3
  81.4 28.7 reduce-scatter.2
  134.2 38.5 all-reduce.5
  182.2 28.7 reduce-scatter.4
  217.0 120.8 all-reduce.7
